TPU v7x, 128 devices: a whole 4x4x4 slice. The times are simulated.
128 devices in a mesh: ctx: 8 (over x, core), exp: 16 (over z, y).
Axes of the slice: x: 4, y: 4, z: 4, core: 2. Of those that a mesh axis runs over, the one named last changes fastest.
Arguments:
- q_act: bfloat16 [2048, 4096], P('ctx', 'exp'), may hold values from -6 to 6
- k_act: bfloat16 [2048, 4096], P('ctx', 'exp'), may hold values from -6 to 6
- v_act: bfloat16 [2048, 4096], P('ctx', 'exp'), may hold values from -6 to 6
- log_forget: float32 [32, 2048], P('exp', 'ctx'), may hold values from -1 to 0
- attn_gain: float32 [4096], P('exp'), may hold values from 0.1 to 1.9
- w_out: bfloat16 [4096, 6144], P('exp'), may hold values from -0.09375 to 0.09375
- resid: bfloat16 [2048, 6144], P(('ctx', 'exp')), may hold values from -6 to 6
- mlp_gain: float32 [6144], replicated, may hold values from 0.1 to 1.9
- gate_w: bfloat16 [16, 4608, 6144], P('exp', 'ctx'), may hold values from -0.078125 to 0.078125
- up_w: bfloat16 [16, 4608, 6144], P('exp', 'ctx'), may hold values from -0.078125 to 0.078125
- down_w: bfloat16 [16, 4608, 6144], P('exp', 'ctx'), may hold values from -0.0625 to 0.0625
- expert_ids: int32 [2048, 2], P(('ctx', 'exp')), may hold values from 0 to 7, all different within a row; in each aligned block of 16 rows (0 to 15, 16 to 31, ...) at most 6 rows name the same one
- gate_codes: int32 [2048, 2], P(('ctx', 'exp')), may hold values from 1 to 1023
Outputs:
- layer_out: bfloat16 [2048, 6144], P(('ctx', 'exp'))
Inputs may be any that keep to these rules, and one draw needn't show every extreme that they name: `expert_ids`: each row names two different experts. In the rows of one device (aligned blocks of 16 rows) no expert is named more than 6 times.
All inputs are finite; a program needn't handle non-finite values.
Results may differ from a plain program's by a relative error of at most 0.02.
Values may be sent and summed in bfloat16 or wider, within the bound.
No kernel may reach another device: no remote copies, remote signals or barrier semaphores. Data moves between devices by JAX's collectives and lax.ppermute only.
A program may use at most 128 MiB of HBM per device.

v0:
```python
import jax
import jax.numpy as jnp
from jax import lax
from jax.sharding import PartitionSpec as P

D = 6144
HEAD_DIM = 128
EXPERTS = 8
BLOCK = 256


EPS = 1e-06


def passed_along(value, axis, steps):
    count = lax.axis_size(axis)
    initial, last = (max(0, -steps), min(count, count - steps))
    return lax.ppermute(value, axis, [(source, source + steps) for source in range(initial, last)])


def slot_tables(ids, codes, experts, capacity):
    rows = ids.shape[0]
    width = ids.shape[1]
    flat = ids.reshape(-1)
    onehot = (flat[:, None] == jnp.arange(experts, dtype=jnp.int32)[None, :]).astype(jnp.int32)
    before = jnp.cumsum(onehot, axis=0) - onehot
    slot = jnp.sum(before * onehot, axis=1)
    target = flat * capacity + slot
    assign = (target[None, :] == jnp.arange(experts * capacity, dtype=jnp.int32)[:, None]).astype(
        jnp.float32
    )
    assign = assign.reshape(experts * capacity, rows, width)
    dispatch = jnp.sum(assign, axis=2)
    route = codes.astype(jnp.float32)
    route = route / jnp.sum(route, axis=1, keepdims=True)
    combine = jnp.einsum("srk,rk->rs", assign, route, precision=lax.Precision.HIGHEST)
    return (dispatch, combine)


def shards(
    q_act,
    k_act,
    v_act,
    log_forget,
    attn_gain,
    w_out,
    resid,
    mlp_gain,
    gate_w,
    up_w,
    down_w,
    expert_ids,
    gate_codes,
):
    tok_ctx = q_act.shape[0]
    head_count = log_forget.shape[0]
    nblocks = tok_ctx // BLOCK
    scale = HEAD_DIM ** (-0.5)
    query_blk = q_act.reshape(nblocks, BLOCK, head_count, HEAD_DIM)
    key_blk = k_act.reshape(nblocks, BLOCK, head_count, HEAD_DIM)
    value_blk = v_act.reshape(nblocks, BLOCK, head_count, HEAD_DIM)
    rates = log_forget.reshape(head_count, nblocks, BLOCK)
    cumul = jnp.cumsum(rates, axis=2)
    positions = jnp.arange(BLOCK)
    causal = positions[:, None] >= positions[None, :]
    differ = jnp.where(causal, cumul[..., :, None] - cumul[..., None, :], 0.0)
    decay = jnp.where(causal, jnp.exp(differ), 0.0)
    scores = (
        jnp.einsum("nihd,njhd->hnij", query_blk, key_blk, preferred_element_type=jnp.float32)
        * scale
        * decay
    )
    intra = jnp.einsum(
        "hnij,njhd->hnid",
        scores.astype(jnp.bfloat16),
        value_blk,
        preferred_element_type=jnp.float32,
    )
    block_ends = cumul[..., -1]
    fading = jnp.exp(block_ends[..., None] - cumul).transpose(1, 2, 0)
    key_faded = key_blk.astype(jnp.float32) * fading[..., None]
    updates = jnp.einsum(
        "njhd,njhe->nhde", key_faded, value_blk.astype(jnp.float32), precision=lax.Precision.HIGHEST
    )

    def chain(carry, pieces):
        block_gain, update = pieces
        return (block_gain[:, None, None] * carry + update, carry)

    start_state = jnp.zeros((head_count, HEAD_DIM, HEAD_DIM), jnp.float32)
    shard_state, entering = lax.scan(chain, start_state, (jnp.exp(block_ends).T, updates))
    prior_log = jnp.cumsum(block_ends, axis=1) - block_ends
    shard_log = jnp.sum(block_ends, axis=1)
    incoming = jnp.zeros_like(shard_state)
    for section_num in range(lax.axis_size("ctx") - 1):
        leaving = jnp.exp(shard_log)[:, None, None] * incoming + shard_state
        incoming = passed_along(leaving.astype(jnp.bfloat16), "ctx", 1).astype(leaving.dtype)
    states_in = (
        entering.transpose(1, 0, 2, 3) + jnp.exp(prior_log)[..., None, None] * incoming[:, None]
    )
    inter = jnp.einsum(
        "nihd,hnde->hnie", query_blk.astype(jnp.float32), states_in, precision=lax.Precision.HIGHEST
    )
    heads_out = intra + scale * jnp.exp(cumul)[..., None] * inter
    meansq = jnp.mean(heads_out * heads_out, axis=3, keepdims=True)
    normed = heads_out * lax.rsqrt(meansq + EPS)
    normed = normed.transpose(1, 2, 0, 3).reshape(tok_ctx, head_count * HEAD_DIM)
    attn_out = (normed * attn_gain).astype(jnp.bfloat16)
    tok_dev = resid.shape[0]
    part_rows = attn_out
    proj = lax.psum_scatter(
        jnp.dot(part_rows, w_out, preferred_element_type=jnp.float32).astype(jnp.bfloat16),
        "exp",
        scatter_dimension=0,
        tiled=True,
    ).astype(jnp.float32)
    mid = (resid.astype(jnp.float32) + proj).astype(jnp.bfloat16)
    mid_f = mid.astype(jnp.float32)
    mixed_in = (
        mid_f * lax.rsqrt(jnp.mean(mid_f * mid_f, axis=1, keepdims=True) + EPS) * mlp_gain
    ).astype(jnp.bfloat16)
    capacity = 3 * tok_dev // 8
    dispatch, combine = slot_tables(expert_ids, gate_codes, EXPERTS, capacity)
    slots = jnp.dot(
        dispatch.astype(jnp.bfloat16), mixed_in, preferred_element_type=jnp.float32
    ).astype(jnp.bfloat16)
    slots = slots.reshape(EXPERTS, capacity, D)
    exp_count = lax.axis_size("exp")
    ctx_count = lax.axis_size("ctx")
    split_count = exp_count // EXPERTS
    outgoing = jnp.repeat(slots, split_count, axis=0)
    gate_rows = gate_w[0]
    up_rows = up_w[0]
    down_rows = down_w[0]
    widened = jnp.broadcast_to(outgoing[None], (ctx_count, exp_count, capacity, D))
    widened = widened.reshape(ctx_count * exp_count, capacity, D)
    rows_in = lax.all_to_all(widened, ("ctx", "exp"), split_axis=0, concat_axis=0, tiled=True)
    gate = jnp.einsum("...c,fc->...f", rows_in, gate_rows, preferred_element_type=jnp.float32)
    upper = jnp.einsum("...c,fc->...f", rows_in, up_rows, preferred_element_type=jnp.float32)
    hidden = (jax.nn.silu(gate) * upper).astype(jnp.bfloat16)
    hidden_flat = hidden.reshape(ctx_count * exp_count * capacity, hidden.shape[-1])
    part_rows = hidden_flat
    summed = lax.psum_scatter(
        jnp.dot(part_rows, down_rows, preferred_element_type=jnp.float32).astype(jnp.bfloat16),
        "ctx",
        scatter_dimension=0,
        tiled=True,
    ).astype(jnp.float32)
    returned = lax.all_to_all(
        summed.reshape(exp_count, capacity, D).astype(jnp.bfloat16),
        "exp",
        split_axis=0,
        concat_axis=0,
        tiled=True,
    ).astype(jnp.float32)
    outputs = jnp.sum(returned.reshape(EXPERTS, split_count, capacity, D), axis=1).reshape(
        EXPERTS * capacity, D
    )
    moe = jnp.dot(
        combine, outputs, precision=lax.Precision.HIGHEST, preferred_element_type=jnp.float32
    )
    return (mid_f + moe).astype(jnp.bfloat16)


def solution(mesh):
    placed = (
        P("ctx", "exp"),
        P("ctx", "exp"),
        P("ctx", "exp"),
        P("exp", "ctx"),
        P("exp"),
        P("exp", None),
        P(("ctx", "exp"), None),
        P(),
        P("exp", "ctx", None),
        P("exp", "ctx", None),
        P("exp", "ctx", None),
        P(("ctx", "exp"), None),
        P(("ctx", "exp"), None),
    )
    return jax.shard_map(
        shards, mesh=mesh, in_specs=placed, out_specs=P(("ctx", "exp"), None), check_vma=False
    )
```

profile of v0, /device:TPU:3, one launch (start us, length us, event | category | flops | bytes accessed | tf_op | source)
XLA Modules:
  0.0 465.0 jit_solution(17906314848441786)
XLA Ops:
  6.5 0.8 reshape.289
  7.4 0.6 reduce-window.6
  8.0 0.2 slice_reduce_fusion
  8.2 0.1 copy.102
  8.3 0.2 reduce-window.9
  8.5 0.1 copy.83
  8.6 0.6 subtract_exponential_fusion
  9.2 0.1 copy.88
  9.3 1.0 copy.103
  10.3 1.2 add_convert_fusion.7
  11.5 3.7 collective-permute-start
  15.2 1.3 collective-permute-done
  16.5 0.1 add_convert_fusion.6
  16.6 4.3 collective-permute-start.1
  20.9 1.3 collective-permute-done.1
  22.2 0.1 add_convert_fusion.5
  22.3 4.3 collective-permute-start.2
  26.6 1.3 collective-permute-done.2
  27.9 0.7 add_convert_fusion.4
  28.6 4.3 collective-permute-start.3
  32.9 1.6 collective-permute-done.3
  34.5 0.9 add_convert_fusion.3
  35.4 4.3 collective-permute-start.4
  39.7 0.6 exponential_multiply_fusion
  40.3 0.7 collective-permute-done.4
  41.0 0.1 add_convert_fusion.2
  41.1 4.3 collective-permute-start.5
  45.3 0.7 iota_compare_fusion
  46.0 0.7 collective-permute-done.5
  46.7 0.7 add_convert_fusion.1
  47.4 4.3 collective-permute-start.6
  51.6 1.4 fusion.16
  53.1 0.2 collective-permute-done.6
  53.2 1.4 multiply_reduce_fusion
  54.6 0.8 fusion.24
  55.4 2.7 convolution_convert_fusion.1
  58.2 0.6 copy-done.5
  58.8 0.1 copy.92
  58.9 0.1 eq.30
  59.1 0.2 select_reduce_fusion
  59.3 0.1 reduce_sum.62
  59.4 0.1 copy.93
  59.5 0.1 convert_reduce_fusion.1
  59.5 76.0 %reduce-scatter.3.cloned.1.call-done = bf16[16,6144]{1,0:T(8,128)(2,1)} async-done(((bf16[256,6144]{1,0:T(8,128)(2,1)}), bf16[16,6144]{1,0:T(8,128)(2,1)}) %reduce-scatter.3.cloned.1.call-update) | async-done | bytes 196624 | tf_op jit(solution)/shard_map/reduce_scatter | solution.py:111
  135.6 1.1 fusion.21
  136.7 1.3 convolution_convert_fusion.2
  138.0 0.2 reshape.298
  138.2 0.2 broadcast_in_dim.25
  138.4 6.1 %broadcast_in_dim.27 = bf16[8,16,6,6144]{3,2,1,0:T(8,128)(2,1)} broadcast(bf16[16,6,6144]{2,1,0:T(8,128)(2,1)S(1)} %bitcast.106), dimensions={1,2,3} | broadcast | bytes 10616832 | tf_op jit(solution)/shard_map/broadcast_in_dim | solution.py:135
  144.5 153.9 %all_to_all.10 = bf16[128,6,6144]{2,1,0:T(8,128)(2,1)S(1)} all-to-all(bf16[128,6,6144]{2,1,0:T(8,128)(2,1)} %bitcast.105), channel_id=1, replica_groups=mesh['ctx'=8,'exp'=16] {'ctx','exp'}, dimensions={0} | all-to-all | bytes 18874368 | tf_op jit(solution)/shard_map/all_to_all | solution.py:137
  298.4 27.0 %fusion.1 = f32[128,6,576]{0,2,1:T(8,128)S(1)} fusion(bf16[1,576,6144]{2,1,0:T(8,128)(2,1)} %param.22, bf16[128,6,6144]{2,1,0:T(8,128)(2,1)S(1)} %all_to_all.10), kind=kOutput, calls=%fused_computation.3 | convolution fusion | flops 5435817984 | bytes 18284544 | tf_op jit(solution)/shard_map/...c,fc->...f/dot_general | solution.py:139
  325.5 15.5 %multiply_convert_fusion = bf16[128,6,576]{0,2,1:T(8,128)(2,1)S(1)} fusion(f32[128,6,576]{0,2,1:T(8,128)S(1)} %fusion.1, bf16[1,576,6144]{2,1,0:T(8,128)(2,1)S(1)} %bitcast.117, bf16[128,6,6144]{2,1,0:T(8,128)(2,1)S(1)} %all_to_all.10), kind=kOutput, calls=%fused_computation.13 | convolution fusion | flops 5438472192 | bytes 19169280 | tf_op jit(solution)/shard_map/...c,fc->...f/dot_general | solution.py:138
  341.0 1.3 copy.96
  342.3 0.6 reshape.300
  343.0 12.6 %convolution_convert_fusion = bf16[768,6144]{1,0:T(8,128)(2,1)} fusion(bf16[768,576]{1,0:T(8,128)(2,1)S(1)} %reshape.300, bf16[1,576,6144]{2,1,0:T(8,128)(2,1)} %param.23), kind=kOutput, calls=%fused_computation | convolution fusion | flops 5440536576 | bytes 17399808 | tf_op jit(solution)/shard_map/dot_general | solution.py:144
  355.6 57.9 %reduce-scatter.5.cloned.1.call-done = bf16[96,6144]{1,0:T(8,128)(2,1)} async-done(((bf16[768,6144]{1,0:T(8,128)(2,1)}), bf16[96,6144]{1,0:T(8,128)(2,1)}) %reduce-scatter.5.cloned.1.call-update) | async-done | bytes 1179664 | tf_op jit(solution)/shard_map/reduce_scatter | solution.py:143
  413.5 2.4 convert_element_type.136
  415.9 6.7 %all-to-all-start.1 = ((bf16[16,6,6144]{2,1,0:T(8,128)(2,1)}), bf16[16,6,6144]{2,1,0:T(8,128)(2,1)}, u32[]{:S(2)}, u32[]{:S(2)}) async-start(bf16[16,6,6144]{2,1,0:T(8,128)(2,1)} %convert_element_type.136), calls=%async_computation.3 | async-start | bytes 3145728 | tf_op jit(solution)/shard_map/all_to_all | solution.py:149
  422.7 0.1 copy.99
  422.8 0.2 fusion.49
  423.0 26.7 %all-to-all-done.1 = bf16[16,6,6144]{2,1,0:T(8,128)(2,1)} async-done(((bf16[16,6,6144]{2,1,0:T(8,128)(2,1)}), bf16[16,6,6144]{2,1,0:T(8,128)(2,1)}, u32[]{:S(2)}, u32[]{:S(2)}) %all-to-all-start.1) | async-done | bytes 1179680 | tf_op jit(solution)/shard_map/all_to_all | solution.py:149
  449.7 3.1 convert_reduce_fusion
  452.7 2.6 reshape.303
  455.3 2.6 fusion.7
  (37 shorter events, 0.5 us)
Async XLA Ops:
  6.5 48.9 %copy-start = (bf16[256,6144]{1,0:T(8,128)(2,1)S(1)}, bf16[256,6144]{1,0:T(8,128)(2,1)}, u32[]{:S(2)}) copy-start(bf16[256,6144]{1,0:T(8,128)(2,1)} %param.18) | copy-start | bytes 9437188
  6.5 129.1 %reduce-scatter.3.cloned.1.call-start = ((), (), s32[]{:S(2)}) async-start(), calls=%async_computation.4 | async-start | bytes 3342336 | tf_op jit(solution)/shard_map/reduce_scatter | solution.py:111
  11.5 5.0 %collective-permute-start = (bf16[2,128,128]{2,1,0:T(8,128)(2,1)S(1)}, bf16[2,128,128]{2,1,0:T(8,128)(2,1)S(1)}, u32[]{:S(2)}, u32[]{:S(2)}) collective-permute-start(bf16[2,128,128]{2,1,0:T(8,128)(2,1)S(1)} %get-tuple-element.26), channel_id=1, source_target_pairs={{0,16},{16,32},{32,48},{48,64},{64,80},{80,96},{96,112},{1,17},{17... | collective-permute-start | bytes 196616 | tf_op jit(solution)/shard_map/ppermute | solution.py:18
  16.6 5.6 %collective-permute-start.1 = (bf16[2,128,128]{2,1,0:T(8,128)(2,1)S(1)}, bf16[2,128,128]{2,1,0:T(8,128)(2,1)S(1)}, u32[]{:S(2)}, u32[]{:S(2)}) collective-permute-start(bf16[2,128,128]{2,1,0:T(8,128)(2,1)S(1)} %add_convert_fusion.6), channel_id=1, source_target_pairs={{0,16},{16,32},{32,48},{48,64},{64,80},{80,96},{96,112},{1,17},{17... | collective-permute-start | bytes 196616 | tf_op jit(solution)/shard_map/ppermute | solution.py:18
  22.3 5.6 %collective-permute-start.2 = (bf16[2,128,128]{2,1,0:T(8,128)(2,1)S(1)}, bf16[2,128,128]{2,1,0:T(8,128)(2,1)S(1)}, u32[]{:S(2)}, u32[]{:S(2)}) collective-permute-start(bf16[2,128,128]{2,1,0:T(8,128)(2,1)S(1)} %add_convert_fusion.5), channel_id=1, source_target_pairs={{0,16},{16,32},{32,48},{48,64},{64,80},{80,96},{96,112},{1,17},{17... | collective-permute-start | bytes 196616 | tf_op jit(solution)/shard_map/ppermute | solution.py:18
  28.6 5.9 %collective-permute-start.3 = (bf16[2,128,128]{2,1,0:T(8,128)(2,1)}, bf16[2,128,128]{2,1,0:T(8,128)(2,1)}, u32[]{:S(2)}, u32[]{:S(2)}) collective-permute-start(bf16[2,128,128]{2,1,0:T(8,128)(2,1)} %add_convert_fusion.4), channel_id=1, source_target_pairs={{0,16},{16,32},{32,48},{48,64},{64,80},{80,96},{96,112},{1,17},{17... | collective-permute-start | bytes 196616 | tf_op jit(solution)/shard_map/ppermute | solution.py:18
  35.4 5.6 %collective-permute-start.4 = (bf16[2,128,128]{2,1,0:T(8,128)(2,1)S(1)}, bf16[2,128,128]{2,1,0:T(8,128)(2,1)S(1)}, u32[]{:S(2)}, u32[]{:S(2)}) collective-permute-start(bf16[2,128,128]{2,1,0:T(8,128)(2,1)S(1)} %add_convert_fusion.3), channel_id=1, source_target_pairs={{0,16},{16,32},{32,48},{48,64},{64,80},{80,96},{96,112},{1,17},{17... | collective-permute-start | bytes 196616 | tf_op jit(solution)/shard_map/ppermute | solution.py:18
  41.1 5.6 %collective-permute-start.5 = (bf16[2,128,128]{2,1,0:T(8,128)(2,1)S(1)}, bf16[2,128,128]{2,1,0:T(8,128)(2,1)S(1)}, u32[]{:S(2)}, u32[]{:S(2)}) collective-permute-start(bf16[2,128,128]{2,1,0:T(8,128)(2,1)S(1)} %add_convert_fusion.2), channel_id=1, source_target_pairs={{0,16},{16,32},{32,48},{48,64},{64,80},{80,96},{96,112},{1,17},{17... | collective-permute-start | bytes 196616 | tf_op jit(solution)/shard_map/ppermute | solution.py:18
  47.4 5.9 %collective-permute-start.6 = (bf16[2,128,128]{2,1,0:T(8,128)(2,1)}, bf16[2,128,128]{2,1,0:T(8,128)(2,1)}, u32[]{:S(2)}, u32[]{:S(2)}) collective-permute-start(bf16[2,128,128]{2,1,0:T(8,128)(2,1)} %add_convert_fusion.1), channel_id=1, source_target_pairs={{0,16},{16,32},{32,48},{48,64},{64,80},{80,96},{96,112},{1,17},{17... | collective-permute-start | bytes 196616 | tf_op jit(solution)/shard_map/ppermute | solution.py:18
  58.1 0.7 copy-start.5
  58.1 77.5 %copy-start.2 = (bf16[16,6144]{1,0:T(8,128)(2,1)S(1)}, bf16[16,6144]{1,0:T(8,128)(2,1)}, u32[]{:S(2)}) copy-start(bf16[16,6144]{1,0:T(8,128)(2,1)} %param.19) | copy-start | bytes 589828
  58.1 78.6 %copy-start.4 = (f32[6144]{0:T(1024)S(1)}, f32[6144]{0:T(1024)}, u32[]{:S(2)}) copy-start(f32[6144]{0:T(1024)} %param.20) | copy-start | bytes 73732
  58.2 355.3 %reduce-scatter.5.cloned.1.call-start = ((), (), s32[]{:S(2)}) async-start(), calls=%async_computation.5 | async-start | bytes 10616832 | tf_op jit(solution)/shard_map/reduce_scatter | solution.py:143
  144.5 180.9 %slice-start = ((s8[7077888]{0:T(1024)(128)(4,1)}), s8[4194304]{0:T(1024)(128)(4,1)S(1)}, s32[]{:S(2)}) async-start(s8[7077888]{0:T(1024)(128)(4,1)} %bitcast.116), calls=%async_computation.6 | async-start | bytes 8388608
  298.4 27.1 %slice-start.1 = ((s8[7077888]{0:T(1024)(128)(4,1)}), s8[2883584]{0:T(1024)(128)(4,1)S(1)}, s32[]{:S(2)}) async-start(s8[7077888]{0:T(1024)(128)(4,1)} %bitcast.116), calls=%async_computation.7 | async-start | bytes 5767168
  355.6 67.0 %copy-start.6 = (s32[16,2]{0,1:T(2,128)S(1)}, s32[16,2]{0,1:T(2,128)}, u32[]{:S(2)}) copy-start(s32[16,2]{0,1:T(2,128)} %param.25) | copy-start | bytes 388
  415.9 33.8 %all-to-all-start.1 = ((bf16[16,6,6144]{2,1,0:T(8,128)(2,1)}), bf16[16,6,6144]{2,1,0:T(8,128)(2,1)}, u32[]{:S(2)}, u32[]{:S(2)}) async-start(bf16[16,6,6144]{2,1,0:T(8,128)(2,1)} %convert_element_type.136), calls=%async_computation.3 | async-start | bytes 3145728 | tf_op jit(solution)/shard_map/all_to_all | solution.py:149
  422.6 32.7 %copy-start.3 = (bf16[16,6144]{1,0:T(8,128)(2,1)S(1)}, bf16[16,6144]{1,0:T(8,128)(2,1)}, u32[]{:S(2)}) copy-start(bf16[16,6144]{1,0:T(8,128)(2,1)} %reduce-scatter.3.cloned.1.call-done) | copy-start | bytes 589828
  422.8 35.1 %copy-start.1 = (bf16[256,6144]{1,0:T(8,128)(2,1)S(1)}, bf16[256,6144]{1,0:T(8,128)(2,1)}, u32[]{:S(2)}) copy-start(bf16[256,6144]{1,0:T(8,128)(2,1)} %param.18) | copy-start | bytes 9437188
Sparse Core Ops, SparseCore 0:
  58.3 77.2 reduce-scatter.2
  355.7 57.7 reduce-scatter.4
where the time goes:
time: 470 us; the launch traced here: 465 us
  waiting for transfers between devices  168 us (36%)
  blocking collectives  154 us (33%)
  matrix products  65.9 us (14%)
  starting transfers between devices  36 us (8%)
  local copies, waits for them, and re-layouts  17 us (4%)
  between operations  13.9 us (3%)
  other arithmetic  10.7 us (2%)
    all_to_all x1, blocking collectives, shards(): lax.all_to_all(widened, ('ctx', 'exp'), split_axis=0, concat_axis=0, tile...  154 us
    reduce_scatter x1, waiting for transfers between devices, shards(): lax.psum_scatter(jnp.dot(part_rows, w_out, preferred_element_type=jnp.flo...  76 us
    reduce_scatter x1, waiting for transfers between devices, shards(): lax.psum_scatter(jnp.dot(part_rows, down_rows, preferred_element_type=jnp...  57.9 us
    ppermute x7, starting transfers between devices, passed_along(): lax.ppermute(value, axis, [(source, source + steps) for source in range(i...  29.3 us
    dot_general x1, matrix products, shards(): jnp.einsum('...c,fc->...f', rows_in, up_rows, preferred_element_type=jnp....  27 us
    all_to_all x1, waiting for transfers between devices, shards(): lax.all_to_all(summed.reshape(exp_count, capacity, D).astype(jnp.bfloat16...  26.7 us
    dot_general x1, matrix products, shards(): jnp.einsum('...c,fc->...f', rows_in, gate_rows, preferred_element_type=jn...  15.5 us
    dot_general x1, matrix products, shards(): jnp.dot(part_rows, down_rows, preferred_element_type=jnp.float32)  12.6 us
  transfers between devices with their start and end apart: 10, of which 10 were waited for; matrix products, arithmetic and copies ran while one was open for 1% of the time, Pallas kernels for 0%

commit v1 on v0

v1 whole, which is shorter than its diff:
```python
import jax
import jax.numpy as jnp
from jax import lax
from jax.experimental import pallas as pl
from jax.experimental.pallas import tpu as pltpu
from jax.sharding import PartitionSpec as P

D = 6144
HEAD_DIM = 128
EXPERTS = 8
BLOCK = 256
N_CTX = 8
N_EXP = 16
RING = 4
CAP = 6
ROWS = N_EXP * CAP
HALF = ROWS // 2
COLS = D // N_EXP
EPS = 1e-06
F32 = jnp.float32
BF16 = jnp.bfloat16
VMEM_BYTES = 56 * 1024 * 1024


def along_x(value, steps):
    pairs = [(c, ((c // 2 + steps) % RING) * 2 + c % 2) for c in range(N_CTX)]
    return lax.ppermute(value, "ctx", pairs)


def other_core(value):
    return lax.ppermute(value, "ctx", [(c, c ^ 1) for c in range(N_CTX)])


def forward(value, steps):
    return lax.ppermute(value, "ctx", [(c, c + steps) for c in range(N_CTX - steps)])


def all_to_all_exp(value):
    return lax.all_to_all(value, "exp", split_axis=0, concat_axis=0, tiled=True)


def three_parts(x):
    a = lax.reduce_precision(x, 8, 7)
    b = lax.reduce_precision(x - a, 8, 7)
    c = lax.reduce_precision(x - a - b, 8, 7)
    return a, b, c


def attention(q_act, k_act, v_act, log_forget, attn_gain):
    heads = log_forget.shape[0]
    rows = q_act.shape[0]
    scale = HEAD_DIM ** (-0.5)
    query = q_act.reshape(rows, heads, HEAD_DIM)
    key = k_act.reshape(rows, heads, HEAD_DIM)
    value = v_act.reshape(rows, heads, HEAD_DIM)
    cumul = jnp.cumsum(log_forget, axis=1)
    ends = cumul[:, -1]
    fading = jnp.exp(ends[:, None] - cumul).T
    key_faded = key.astype(F32) * fading[..., None]
    update = jnp.einsum(
        "jhd,jhe->hde", key_faded, value.astype(F32), precision=lax.Precision.HIGHEST
    )
    parts = jnp.stack(three_parts(ends), axis=0).reshape(-1)
    parts = jnp.broadcast_to(
        jnp.pad(parts, (0, 16 - parts.shape[0]))[:, None], (16, HEAD_DIM)
    )
    packed = jnp.concatenate(
        [update.reshape(heads * HEAD_DIM, HEAD_DIM), parts], axis=0
    ).astype(BF16)
    incoming = jnp.zeros((heads, HEAD_DIM, HEAD_DIM), F32)
    passed = jnp.zeros((heads,), F32)
    for steps in range(1, N_CTX):
        got = forward(packed, steps).astype(F32)
        state = got[: heads * HEAD_DIM].reshape(heads, HEAD_DIM, HEAD_DIM)
        incoming = incoming + jnp.exp(passed)[:, None, None] * state
        logs = got[heads * HEAD_DIM : heads * HEAD_DIM + 3 * heads, 0].reshape(3, heads)
        passed = passed + (logs[0] + logs[1] + logs[2])
    positions = jnp.arange(rows)
    causal = positions[:, None] >= positions[None, :]
    differ = jnp.where(causal, cumul[:, :, None] - cumul[:, None, :], 0.0)
    decay = jnp.where(causal, jnp.exp(differ), 0.0)
    scores = (
        jnp.einsum("ihd,jhd->hij", query, key, preferred_element_type=F32) * scale * decay
    )
    intra = jnp.einsum("hij,jhd->hid", scores.astype(BF16), value, preferred_element_type=F32)
    inter = jnp.einsum(
        "ihd,hde->hie", query.astype(F32), incoming, precision=lax.Precision.HIGHEST
    )
    heads_out = intra + scale * jnp.exp(cumul)[..., None] * inter
    meansq = jnp.mean(heads_out * heads_out, axis=2, keepdims=True)
    normed = heads_out * lax.rsqrt(meansq + EPS)
    normed = normed.transpose(1, 0, 2).reshape(rows, heads * HEAD_DIM)
    return (normed * attn_gain).astype(BF16)


def slot_targets(ids):
    flat = ids.reshape(-1)
    onehot = (flat[:, None] == jnp.arange(EXPERTS, dtype=jnp.int32)[None, :]).astype(jnp.int32)
    before = jnp.cumsum(onehot, axis=0) - onehot
    slot = jnp.sum(before * onehot, axis=1)
    return slot.reshape(ids.shape)


def proj_body(a_ref, w_ref, resid_ref, hot_ref, mid_ref, send_ref, acc):
    step = pl.program_id(0)
    part = jnp.dot(
        a_ref[0], w_ref[...].reshape(BLOCK, COLS), preferred_element_type=F32
    )

    @pl.when(step == 0)
    def _():
        acc[...] = part

    @pl.when(step > 0)
    def _():
        acc[...] += part

    @pl.when(step == N_EXP - 1)
    def _():
        mid = (resid_ref[...].astype(F32) + acc[...]).astype(BF16)
        mid_ref[...] = mid
        send_ref[...] = jnp.dot(hot_ref[...], mid, preferred_element_type=F32).astype(BF16)


def project(gathered, w_cols, resid_cols, hot):
    return pl.pallas_call(
        proj_body,
        grid=(N_EXP,),
        in_specs=[
            pl.BlockSpec((1, BLOCK, 256), lambda j: (j, 0, 0)),
            pl.BlockSpec((N_CTX, 1, 32, COLS), lambda j: (0, j, 0, 0)),
            pl.BlockSpec((BLOCK, COLS), lambda j: (0, 0)),
            pl.BlockSpec((N_EXP * ROWS, BLOCK), lambda j: (0, 0)),
        ],
        out_specs=[
            pl.BlockSpec((BLOCK, COLS), lambda j: (0, 0)),
            pl.BlockSpec((N_EXP * ROWS, COLS), lambda j: (0, 0)),
        ],
        out_shape=[
            jax.ShapeDtypeStruct((BLOCK, COLS), BF16),
            jax.ShapeDtypeStruct((N_EXP * ROWS, COLS), BF16),
        ],
        scratch_shapes=[pltpu.VMEM((BLOCK, COLS), F32)],
        compiler_params=pltpu.CompilerParams(vmem_limit_bytes=VMEM_BYTES),
        cost_estimate=pl.CostEstimate(
            flops=2 * BLOCK * 4096 * COLS, bytes_accessed=10_000_000, transcendentals=0
        ),
        name="project",
    )(gathered, w_cols, resid_cols, hot)


def norm_body(got_ref, gain_ref, *out_refs):
    for half, out_ref in enumerate(out_refs):
        rows = pl.ds(half * HALF, HALF)
        total = jnp.zeros((HALF, 1), F32)
        for j in range(N_EXP):
            piece = got_ref[j, rows, :].astype(F32)
            total += jnp.sum(piece * piece, axis=1, keepdims=True)
        factor = lax.rsqrt(total * (1.0 / D) + EPS)
        for j in range(N_EXP):
            cols = pl.ds(j * COLS, COLS)
            piece = got_ref[j, rows, :].astype(F32)
            out_ref[:, cols] = (piece * factor * gain_ref[:, cols]).astype(BF16)


def norm_rows(got, mlp_gain):
    return pl.pallas_call(
        norm_body,
        in_specs=[pl.BlockSpec(memory_space=pltpu.VMEM)] * 2,
        out_specs=[pl.BlockSpec(memory_space=pltpu.VMEM)] * 2,
        out_shape=[jax.ShapeDtypeStruct((HALF, D), BF16)] * 2,
        compiler_params=pltpu.CompilerParams(vmem_limit_bytes=VMEM_BYTES),
        cost_estimate=pl.CostEstimate(
            flops=4 * ROWS * D, bytes_accessed=4 * ROWS * D, transcendentals=0
        ),
        name="norm_rows",
    )(got, mlp_gain.reshape(1, D))


STEPS = 6
WIDE = D // STEPS


def ffn_body(*refs):
    n = 2 * RING
    x_refs = refs[:n]
    gate_ref, up_ref, down_ref = refs[n : n + 3]
    out_refs = refs[n + 3 : 2 * n + 3]
    gate_acc, up_acc, hidden = refs[2 * n + 3 :]
    step = pl.program_id(0)
    dims = (((1,), (1,)), ((), ()))

    @pl.when(step < STEPS)
    def _():
        rows = jnp.concatenate([r[...] for r in x_refs], axis=0)
        gate = lax.dot_general(rows, gate_ref[0], dims, preferred_element_type=F32)
        up = lax.dot_general(rows, up_ref[0], dims, preferred_element_type=F32)

        @pl.when(step == 0)
        def _():
            gate_acc[...] = gate
            up_acc[...] = up

        @pl.when(step > 0)
        def _():
            gate_acc[...] += gate
            up_acc[...] += up

    @pl.when(step == STEPS - 1)
    def _():
        hidden[...] = (jax.nn.silu(gate_acc[...]) * up_acc[...]).astype(BF16)

    @pl.when(step >= STEPS)
    def _():
        out = jnp.dot(hidden[...], down_ref[0], preferred_element_type=F32).astype(BF16)
        for i, out_ref in enumerate(out_refs):
            out_ref[...] = out[i * HALF : (i + 1) * HALF]


def expert_ffn(pieces, gate_w, up_w, down_w):
    n = 2 * RING
    total = n * HALF
    ff = gate_w.shape[1]
    first = lambda i: jnp.minimum(i, STEPS - 1)
    second = lambda i: jnp.maximum(i - STEPS, 0)
    return pl.pallas_call(
        ffn_body,
        grid=(2 * STEPS,),
        in_specs=[pl.BlockSpec((HALF, WIDE), lambda i: (0, first(i)))] * n
        + [pl.BlockSpec((1, ff, WIDE), lambda i: (0, 0, first(i)))] * 2
        + [pl.BlockSpec((1, ff, WIDE), lambda i: (0, 0, second(i)))],
        out_specs=[pl.BlockSpec((HALF, WIDE), lambda i: (0, second(i)))] * n,
        out_shape=[jax.ShapeDtypeStruct((HALF, D), BF16)] * n,
        scratch_shapes=[
            pltpu.VMEM((total, ff), F32),
            pltpu.VMEM((total, ff), F32),
            pltpu.VMEM((total, ff), BF16),
        ],
        compiler_params=pltpu.CompilerParams(vmem_limit_bytes=VMEM_BYTES),
        cost_estimate=pl.CostEstimate(
            flops=6 * total * ff * D,
            bytes_accessed=6 * ff * D + 4 * total * D,
            transcendentals=total * ff,
        ),
        name="expert_ffn",
    )(*pieces, gate_w, up_w, down_w)


def gather_rows(own, way):
    left = along_x(own, 1)
    right = along_x(own, -1)
    far = along_x(left, 1) if way > 0 else along_x(right, -1)
    mine = [own, left, right, far]
    return mine + [other_core(piece) for piece in mine]


def added(*terms):
    total = terms[0].astype(F32)
    for term in terms[1:]:
        total = total + term.astype(F32)
    return total


def scatter_rows(outs, way):
    theirs = [other_core(piece) for piece in outs[RING:]]
    own, left, right, far = [added(a, b) for a, b in zip(outs[:RING], theirs)]
    far = far.astype(BF16)
    if way > 0:
        right = right + along_x(far, 1).astype(F32)
    else:
        left = left + along_x(far, -1).astype(F32)
    from_left = along_x(right.astype(BF16), 1)
    from_right = along_x(left.astype(BF16), -1)
    return added(own, from_left, from_right).astype(BF16)


def shards(
    q_act,
    k_act,
    v_act,
    log_forget,
    attn_gain,
    w_out,
    resid,
    mlp_gain,
    gate_w,
    up_w,
    down_w,
    expert_ids,
    gate_codes,
):
    tok_dev = resid.shape[0]
    slot = slot_targets(expert_ids)
    place = expert_ids * ROWS + lax.axis_index("exp") * CAP + slot
    places = lax.all_gather(place, "exp", axis=0, tiled=True)
    targets = jnp.arange(N_EXP * ROWS, dtype=jnp.int32)
    targets = (targets // (2 * ROWS)) * ROWS + targets % ROWS
    hot = (
        (targets[:, None] == places[None, :, 0]) | (targets[:, None] == places[None, :, 1])
    ).astype(BF16)

    eighth = w_out.shape[0] // N_CTX
    w_part = lax.dynamic_slice_in_dim(w_out, lax.axis_index("ctx") * eighth, eighth, 0)
    early = jnp.concatenate([w_part, resid], axis=0)
    early = early.reshape(eighth + tok_dev, N_EXP, COLS).transpose(1, 0, 2)
    early = all_to_all_exp(early)
    resid_cols = early[:, eighth:].reshape(N_EXP * tok_dev, COLS)
    w_cols = lax.all_gather(early[:, :eighth], "ctx", axis=0)

    attn_out = attention(q_act, k_act, v_act, log_forget, attn_gain)
    gathered = all_to_all_exp(jnp.broadcast_to(attn_out[None], (N_EXP,) + attn_out.shape))
    mid_cols, send = project(gathered, w_cols, resid_cols, hot)
    got = all_to_all_exp(send.reshape(N_EXP, ROWS, COLS))
    halves = norm_rows(got, mlp_gain)
    mid_own = all_to_all_exp(mid_cols.reshape(N_EXP, tok_dev, COLS))

    sums = []
    for way, half in zip((1, -1), halves):
        outs = expert_ffn(gather_rows(half, way), gate_w, up_w, down_w)
        sums.append(scatter_rows(outs, way))
    back = jnp.concatenate(sums, axis=0).reshape(N_EXP, CAP, D)
    returned = all_to_all_exp(back).astype(F32)
    outputs = jnp.sum(returned.reshape(EXPERTS, 2, CAP, D), axis=1).reshape(EXPERTS * CAP, D)

    own_place = (expert_ids * CAP + slot)[:, :, None]
    route = gate_codes.astype(F32)
    route = route / jnp.sum(route, axis=1, keepdims=True)
    slots = jnp.arange(EXPERTS * CAP, dtype=jnp.int32)[None, None, :]
    combine = jnp.sum(jnp.where(own_place == slots, route[:, :, None], 0.0), axis=1)
    moe = jnp.dot(combine, outputs, precision=lax.Precision.HIGHEST, preferred_element_type=F32)
    mid_f = mid_own.transpose(1, 0, 2).reshape(tok_dev, D).astype(F32)
    return (mid_f + moe).astype(BF16)


def solution(mesh):
    placed = (
        P("ctx", "exp"),
        P("ctx", "exp"),
        P("ctx", "exp"),
        P("exp", "ctx"),
        P("exp"),
        P("exp", None),
        P(("ctx", "exp"), None),
        P(),
        P("exp", "ctx", None),
        P("exp", "ctx", None),
        P("exp", "ctx", None),
        P(("ctx", "exp"), None),
        P(("ctx", "exp"), None),
    )
    return jax.shard_map(
        shards, mesh=mesh, in_specs=placed, out_specs=P(("ctx", "exp"), None), check_vma=False
    )
```

time: 470 us -> 322 us (0.69)
  blocking collectives: 154 us -> 56.4 us
  waiting for transfers between devices: 168 us -> 74 us
  matrix products: 65.9 us -> 3.69 us
  Pallas kernels: 0 us -> 57.1 us
  starting transfers between devices: 36 us -> 87.5 us
    all_to_all x1, blocking collectives: 154 us -> 17.8 us  [all_to_all_exp(): return lax.all_to_all(value, 'exp', split_axis=0, concat_axis=0, tiled=True)]
    reduce_scatter x2 -> x0, waiting for transfers between devices: 134 us -> none  [the longest x1 76 us: shards(): lax.psum_scatter(jnp.dot(part_rows, w_out, preferred_element_type=jnp.flo...]
    dot_general x9 -> x3, matrix products: 63.2 us -> 1.07 us  [the longest x1 0.44 us: attention(): jnp.einsum('hij,jhd->hid', scores.astype(BF16), value, preferred_element_...]
    pallas_call x0 -> x4, Pallas kernels: none -> 57.1 us  [the longest x2 41.7 us: expert_ffn(): pl.pallas_call(ffn_body, grid=(2 * STEPS,), in_specs=[pl.BlockSpec((HALF,...]
    all_gather x0 -> x1, blocking collectives: none -> 38.6 us  [shards(): places = lax.all_gather(place, 'exp', axis=0, tiled=True)]
    ppermute x7 -> x35, starting transfers between devices: 29.3 us -> 67.7 us  [the longest x16 32.1 us: other_core(): return lax.ppermute(value, 'ctx', [(c, c ^ 1) for c in range(N_CTX)])]
    ppermute x7 -> x35, waiting for transfers between devices: 7.03 us -> 44.1 us  [the longest x12 38.4 us: along_x(): return lax.ppermute(value, 'ctx', pairs)]
    all_to_all x1 -> x4, starting transfers between devices: 6.73 us -> 19.7 us  [all_to_all_exp(): return lax.all_to_all(value, 'exp', split_axis=0, concat_axis=0, tiled=True)]
  transfers between devices with their start and end apart: 10 -> 40, of which waited for: 10 -> 11; matrix products, arithmetic and copies ran while one was open for 1% -> 3% of each run, Pallas kernels for 0% -> 13%
where the time goes in v1:
time: 322 us; the launch traced here: 315 us
  starting transfers between devices  87.5 us (27%)
  waiting for transfers between devices  74 us (23%)
  Pallas kernels  57.1 us (18%)
  blocking collectives  56.4 us (18%)
  local copies, waits for them, and re-layouts  15.2 us (5%)
  between operations  14 us (4%)
  other arithmetic  7.4 us (2%)
  matrix products  3.69 us (1%)
    pallas_call x2, Pallas kernels, expert_ffn(): pl.pallas_call(ffn_body, grid=(2 * STEPS,), in_specs=[pl.BlockSpec((HALF,...  41.7 us
    all_gather x1, blocking collectives, shards(): places = lax.all_gather(place, 'exp', axis=0, tiled=True)  38.6 us
    ppermute x12, waiting for transfers between devices, along_x(): return lax.ppermute(value, 'ctx', pairs)  38.4 us
    ppermute x16, starting transfers between devices, other_core(): return lax.ppermute(value, 'ctx', [(c, c ^ 1) for c in range(N_CTX)])  32.1 us
    all_to_all x4, waiting for transfers between devices, all_to_all_exp(): return lax.all_to_all(value, 'exp', split_axis=0, concat_axis=0, tiled=True)  29.9 us
    ppermute x12, starting transfers between devices, along_x(): return lax.ppermute(value, 'ctx', pairs)  22.4 us
    all_to_all x4, starting transfers between devices, all_to_all_exp(): return lax.all_to_all(value, 'exp', split_axis=0, concat_axis=0, tiled=True)  19.7 us
    all_to_all x1, blocking collectives, all_to_all_exp(): return lax.all_to_all(value, 'exp', split_axis=0, concat_axis=0, tiled=True)  17.8 us
  transfers between devices with their start and end apart: 40, of which 11 were waited for; matrix products, arithmetic and copies ran while one was open for 3% of the time, Pallas kernels for 13%

profile of v1, /device:TPU:3, one launch (start us, length us, event | category | flops | bytes accessed | tf_op | source)
XLA Modules:
  0.0 315.3 jit_solution(11825671839526983022)
XLA Ops:
  6.5 1.9 copy-done
  8.5 1.0 pad_maximum_fusion.1
  9.5 0.9 copy.187
  10.5 7.9 %all-to-all-start.1 = ((bf16[16,48,384]{2,1,0:T(8,128)(2,1)}), bf16[16,48,384]{2,1,0:T(8,128)(2,1)S(1)}, u32[]{:S(2)}, u32[]{:S(2)}) async-start(bf16[16,48,384]{2,1,0:T(8,128)(2,1)} %copy.187), calls=%async_computation.1 | async-start | bytes 1179648 | tf_op jit(solution)/shard_map/all_to_all | solution.py:39
  18.4 0.6 reduce-window.6
  19.7 9.8 %all-to-all-done.1 = bf16[16,48,384]{2,1,0:T(8,128)(2,1)S(1)} async-done(((bf16[16,48,384]{2,1,0:T(8,128)(2,1)}), bf16[16,48,384]{2,1,0:T(8,128)(2,1)S(1)}, u32[]{:S(2)}, u32[]{:S(2)}) %all-to-all-start.1) | async-done | bytes 589856 | tf_op jit(solution)/shard_map/all_to_all | solution.py:39
  29.4 0.8 slice.198
  31.0 5.1 %collective-permute-start = (bf16[272,128]{0,1:T(8,128)(2,1)S(1)}, bf16[272,128]{0,1:T(8,128)(2,1)S(1)}, u32[]{:S(2)}, u32[]{:S(2)}) collective-permute-start(bf16[272,128]{0,1:T(8,128)(2,1)S(1)} %pad_maximum_fusion.2), channel_id=1, source_target_pairs={{0,16},{16,32},{32,48},{48,64},{64,80},{80,96},{96,112},{1,17},{17... | collective-permute-start | bytes 208904 | tf_op jit(solution)/shard_map/ppermute | solution.py:35
  36.1 2.8 collective-permute-start.1
  39.0 1.9 collective-permute-start.2
  40.9 1.3 collective-permute-start.3
  42.2 0.7 collective-permute-start.4
  42.9 0.7 collective-permute-start.5
  43.6 0.8 collective-permute-done.1
  44.4 0.7 collective-permute-start.6
  45.1 3.3 %collective-permute-done.2 = bf16[272,128]{0,1:T(8,128)(2,1)S(1)} collective-permute-done((bf16[272,128]{0,1:T(8,128)(2,1)S(1)}, bf16[272,128]{0,1:T(8,128)(2,1)S(1)}, u32[]{:S(2)}, u32[]{:S(2)}) %collective-permute-start.2) | collective-permute-done | bytes 69664 | tf_op jit(solution)/shard_map/ppermute | solution.py:35
  48.4 0.4 collective-permute-done.3
  49.4 0.4 fusion.20
  49.8 0.4 fusion.9
  50.5 1.5 broadcast_in_dim.27
  52.0 3.8 %all-to-all-start = ((bf16[16,256,256]{2,1,0:T(8,128)(2,1)}), bf16[16,256,256]{2,1,0:T(8,128)(2,1)S(1)}, u32[]{:S(2)}, u32[]{:S(2)}) async-start(bf16[16,256,256]{2,1,0:T(8,128)(2,1)} %broadcast_in_dim.27), calls=%async_computation | async-start | bytes 4194304 | tf_op jit(solution)/shard_map/all_to_all | solution.py:39
  56.6 38.6 %all-gather.1 = s32[16,16,2]{1,2,0:T(2,128)S(1)} all-gather(s32[1,16,2]{1,2,0:T(2,128)S(1)} %get-tuple-element.56), channel_id=1, replica_groups=mesh['ctx'=8,'exp'=16] {'exp'}, dimensions={0}, use_global_device_ids=true | all-gather | bytes 2176 | tf_op jit(solution)/shard_map/all_gather | solution.py:295
  95.3 1.2 or_convert_fusion.hot_ref
  96.4 0.7 slice.199
  97.1 1.3 copy-done.2
  98.4 12.7 %project.1 = (bf16[256,384]{1,0:T(8,128)(2,1)}, bf16[1536,384]{1,0:T(8,128)(2,1)}) custom-call(bf16[16,256,256]{2,1,0:T(8,128)(2,1)} %copy-done.2, bf16[8,16,32,384]{3,2,1,0:T(8,128)(2,1)} %bitcast.187, bf16[256,384]{1,0:T(8,128)(2,1)} %bitcast.193, bf16[1536,256]{1,0:T(8,128)(2,1)} %or_convert_fusion.hot_ref), custom_call_target="tpu_custom_call" | custom-call | flops 805306368 | bytes 10000000 | tf_op jit(solution)/shard_map/project/pallas_call | solution.py:126
  111.2 17.8 %all_to_all.25.got_ref = bf16[16,96,384]{2,1,0:T(8,128)(2,1)} all-to-all(bf16[16,96,384]{2,1,0:T(8,128)(2,1)} %bitcast.191), channel_id=1, replica_groups=mesh['ctx'=8,'exp'=16] {'exp'}, dimensions={0} | all-to-all | bytes 2359296 | tf_op jit(solution)/shard_map/all_to_all | solution.py:39
  129.0 2.7 norm_rows.1
  131.7 7.4 %collective-permute-start.7 = (bf16[48,6144]{1,0:T(8,128)(2,1)}, bf16[48,6144]{1,0:T(8,128)(2,1)S(1)}, u32[]{:S(2)}, u32[]{:S(2)}) collective-permute-start(bf16[48,6144]{1,0:T(8,128)(2,1)} %get-tuple-element.27.refs_0_), channel_id=1, source_target_pairs={{0,32},{16,48},{32,64},{48,80},{64,96},{80,112},{96,0},{112,16},{1... | collective-permute-start | bytes 1769480 | tf_op jit(solution)/shard_map/ppermute | solution.py:27
  139.1 1.2 collective-permute-start.8
  140.3 6.6 %collective-permute-start.10 = (bf16[48,6144]{1,0:T(8,128)(2,1)}, bf16[48,6144]{1,0:T(8,128)(2,1)S(1)}, u32[]{:S(2)}, u32[]{:S(2)}) collective-permute-start(bf16[48,6144]{1,0:T(8,128)(2,1)} %get-tuple-element.27.refs_0_), channel_id=1, source_target_pairs={{0,16},{16,0},{32,48},{48,32},{64,80},{80,64},{96,112},{112,96},{1... | collective-permute-start | bytes 1769480 | tf_op jit(solution)/shard_map/ppermute | solution.py:31
  146.9 3.0 collective-permute-start.22
  149.8 2.0 collective-permute-start.21
  151.8 10.4 %collective-permute-start.11 = (bf16[48,6144]{1,0:T(8,128)(2,1)S(1)}, bf16[48,6144]{1,0:T(8,128)(2,1)}, u32[]{:S(2)}, u32[]{:S(2)}) collective-permute-start(bf16[48,6144]{1,0:T(8,128)(2,1)S(1)} %collective-permute-done.7.refs_1_), channel_id=1, source_target_pairs={{0,16},{16,0},{32,48},{48,32},{64,80},{80,64},{96,112},{112,96},{1... | collective-permute-start | bytes 1769480 | tf_op jit(solution)/shard_map/ppermute | solution.py:31
  162.3 1.0 collective-permute-done.22.refs_2_
  163.3 2.2 collective-permute-start.23
  165.5 8.4 %collective-permute-start.13 = (bf16[48,6144]{1,0:T(8,128)(2,1)}, bf16[48,6144]{1,0:T(8,128)(2,1)}, u32[]{:S(2)}, u32[]{:S(2)}) collective-permute-start(bf16[48,6144]{1,0:T(8,128)(2,1)} %collective-permute-done.9.refs_3_), channel_id=1, source_target_pairs={{0,16},{16,0},{32,48},{48,32},{64,80},{80,64},{96,112},{112,96},{1... | collective-permute-start | bytes 1769480 | tf_op jit(solution)/shard_map/ppermute | solution.py:31
  174.0 3.5 %all-to-all-start.2 = ((bf16[16,16,384]{2,1,0:T(8,128)(2,1)}), bf16[16,16,384]{2,1,0:T(8,128)(2,1)S(1)}, u32[]{:S(2)}, u32[]{:S(2)}) async-start(bf16[16,16,384]{2,1,0:T(8,128)(2,1)} %bitcast.22), calls=%async_computation.2 | async-start | bytes 393216 | tf_op jit(solution)/shard_map/all_to_all | solution.py:39
  177.5 2.7 collective-permute-start.24
  180.3 0.4 collective-permute-start.25
  180.7 1.1 collective-permute-start.27
  181.9 20.9 %expert_ffn.2 = (bf16[48,6144]{1,0:T(8,128)(2,1)}, bf16[48,6144]{1,0:T(8,128)(2,1)}, bf16[48,6144]{1,0:T(8,128)(2,1)}, bf16[48,6144]{1,0:T(8,128)(2,1)}, bf16[48...) custom-call(bf16[48,6144]{1,0:T(8,128)(2,1)} %get-tuple-element.27.refs_0_, ...), custom_call_target="tpu_custom_call" | custom-call | flops 8153726976 | bytes 30670848 | tf_op jit(solution)/shard_map/expert_ffn/pallas_call | solution.py:226
  202.9 0.5 collective-permute-start.15
  203.5 0.4 collective-permute-start.14
  204.4 0.8 copy-done.28
  205.2 20.8 %expert_ffn.3 = (bf16[48,6144]{1,0:T(8,128)(2,1)}, bf16[48,6144]{1,0:T(8,128)(2,1)}, bf16[48,6144]{1,0:T(8,128)(2,1)}, bf16[48,6144]{1,0:T(8,128)(2,1)}, bf16[48...) custom-call(bf16[48,6144]{1,0:T(8,128)(2,1)} %get-tuple-element.36.refs_0_, ...), custom_call_target="tpu_custom_call" | custom-call | flops 8153726976 | bytes 30670848 | tf_op jit(solution)/shard_map/expert_ffn/pallas_call | solution.py:226
  226.1 0.4 collective-permute-start.29
  227.6 0.8 collective-permute-done.29
  228.9 0.4 collective-permute-done.32
  229.2 1.4 collective-permute-start.17
  230.8 0.8 collective-permute-start.20
  231.6 13.3 %collective-permute-done.17 = bf16[48,6144]{1,0:T(8,128)(2,1)S(1)} collective-permute-done((bf16[48,6144]{1,0:T(8,128)(2,1)S(1)}, bf16[48,6144]{1,0:T(8,128)(2,1)S(1)}, u32[]{:S(2)}, u32[]{:S(2)}) %collective-permute-start.17) | collective-permute-done | bytes 589856 | tf_op jit(solution)/shard_map/ppermute | solution.py:27
  244.9 2.4 collective-permute-start.33
  247.6 11.4 %collective-permute-done.33 = bf16[48,6144]{1,0:T(8,128)(2,1)S(1)} collective-permute-done((bf16[48,6144]{1,0:T(8,128)(2,1)S(1)}, bf16[48,6144]{1,0:T(8,128)(2,1)S(1)}, u32[]{:S(2)}, u32[]{:S(2)}) %collective-permute-start.33) | collective-permute-done | bytes 589856 | tf_op jit(solution)/shard_map/ppermute | solution.py:27
  259.0 1.2 collective-permute-start.18
  260.5 0.8 collective-permute-start.34
  261.3 12.7 %collective-permute-done.18 = bf16[48,6144]{1,0:T(8,128)(2,1)S(1)} collective-permute-done((bf16[48,6144]{1,0:T(8,128)(2,1)S(1)}, bf16[48,6144]{1,0:T(8,128)(2,1)S(1)}, u32[]{:S(2)}, u32[]{:S(2)}) %collective-permute-start.18) | collective-permute-done | bytes 589856 | tf_op jit(solution)/shard_map/ppermute | solution.py:27
  274.3 0.7 copy-done.8
  275.4 1.4 reshape.521
  276.8 4.4 %all-to-all-start.4 = ((bf16[16,6,6144]{2,1,0:T(8,128)(2,1)}), bf16[16,6,6144]{2,1,0:T(8,128)(2,1)S(1)}, u32[]{:S(2)}, u32[]{:S(2)}) async-start(bf16[16,6,6144]{2,1,0:T(8,128)(2,1)} %reshape.521), calls=%async_computation.4 | async-start | bytes 3145728 | tf_op jit(solution)/shard_map/all_to_all | solution.py:39
  281.5 20.1 %all-to-all-done.4 = bf16[16,6,6144]{2,1,0:T(8,128)(2,1)S(1)} async-done(((bf16[16,6,6144]{2,1,0:T(8,128)(2,1)}), bf16[16,6,6144]{2,1,0:T(8,128)(2,1)S(1)}, u32[]{:S(2)}, u32[]{:S(2)}) %all-to-all-start.4) | async-done | bytes 1179680 | tf_op jit(solution)/shard_map/all_to_all | solution.py:39
  301.6 1.5 convert_reduce_fusion
  303.1 2.8 reshape.524
  305.9 2.6 fusion
  (156 shorter events, 7.1 us)
Async XLA Ops:
  6.5 1.9 copy-start
  9.5 8.9 %copy-start.15 = (f32[2,256]{1,0:T(2,128)S(1)}, f32[2,256]{1,0:T(2,128)}, u32[]{:S(2)}) copy-start(f32[2,256]{1,0:T(2,128)} %param.16) | copy-start | bytes 6148
  10.5 19.9 %copy-start.11 = (bf16[256,256]{1,0:T(8,128)(2,1)S(1)}, bf16[256,256]{1,0:T(8,128)(2,1)}, u32[]{:S(2)}) copy-start(bf16[256,256]{1,0:T(8,128)(2,1)} %param.14) | copy-start | bytes 393220
  10.5 20.1 %copy-start.12 = (bf16[256,256]{1,0:T(8,128)(2,1)S(1)}, bf16[256,256]{1,0:T(8,128)(2,1)}, u32[]{:S(2)}) copy-start(bf16[256,256]{1,0:T(8,128)(2,1)} %param.15) | copy-start | bytes 393220
  10.5 19.0 %all-to-all-start.1 = ((bf16[16,48,384]{2,1,0:T(8,128)(2,1)}), bf16[16,48,384]{2,1,0:T(8,128)(2,1)S(1)}, u32[]{:S(2)}, u32[]{:S(2)}) async-start(bf16[16,48,384]{2,1,0:T(8,128)(2,1)} %copy.187), calls=%async_computation.1 | async-start | bytes 1179648 | tf_op jit(solution)/shard_map/all_to_all | solution.py:39
  18.4 78.7 %all-gather.4.cloned.1.call-start = ((), (), s32[]{:S(2)}) async-start(), calls=%async_computation.5 | async-start | bytes 3538944 | tf_op jit(solution)/shard_map/all_gather | solution.py:308
  30.5 18.9 %copy-start.13 = (bf16[256,256]{1,0:T(8,128)(2,1)S(1)}, bf16[256,256]{1,0:T(8,128)(2,1)}, u32[]{:S(2)}) copy-start(bf16[256,256]{1,0:T(8,128)(2,1)} %param.13) | copy-start | bytes 393220
  31.0 11.9 %collective-permute-start = (bf16[272,128]{0,1:T(8,128)(2,1)S(1)}, bf16[272,128]{0,1:T(8,128)(2,1)S(1)}, u32[]{:S(2)}, u32[]{:S(2)}) collective-permute-start(bf16[272,128]{0,1:T(8,128)(2,1)S(1)} %pad_maximum_fusion.2), channel_id=1, source_target_pairs={{0,16},{16,32},{32,48},{48,64},{64,80},{80,96},{96,112},{1,17},{17... | collective-permute-start | bytes 208904 | tf_op jit(solution)/shard_map/ppermute | solution.py:35
  36.1 8.3 %collective-permute-start.1 = (bf16[272,128]{0,1:T(8,128)(2,1)S(1)}, bf16[272,128]{0,1:T(8,128)(2,1)S(1)}, u32[]{:S(2)}, u32[]{:S(2)}) collective-permute-start(bf16[272,128]{0,1:T(8,128)(2,1)S(1)} %pad_maximum_fusion.2), channel_id=1, source_target_pairs={{0,32},{16,48},{32,64},{48,80},{64,96},{80,112},{1,33},{17,49},{33... | collective-permute-start | bytes 208904 | tf_op jit(solution)/shard_map/ppermute | solution.py:35
  39.0 9.4 %collective-permute-start.2 = (bf16[272,128]{0,1:T(8,128)(2,1)S(1)}, bf16[272,128]{0,1:T(8,128)(2,1)S(1)}, u32[]{:S(2)}, u32[]{:S(2)}) collective-permute-start(bf16[272,128]{0,1:T(8,128)(2,1)S(1)} %pad_maximum_fusion.2), channel_id=1, source_target_pairs={{0,48},{16,64},{32,80},{48,96},{64,112},{1,49},{17,65},{33,81},{49... | collective-permute-start | bytes 208904 | tf_op jit(solution)/shard_map/ppermute | solution.py:35
  40.9 7.9 %collective-permute-start.3 = (bf16[272,128]{0,1:T(8,128)(2,1)S(1)}, bf16[272,128]{0,1:T(8,128)(2,1)S(1)}, u32[]{:S(2)}, u32[]{:S(2)}) collective-permute-start(bf16[272,128]{0,1:T(8,128)(2,1)S(1)} %pad_maximum_fusion.2), channel_id=1, source_target_pairs={{0,64},{16,80},{32,96},{48,112},{1,65},{17,81},{33,97},{49,113},{2... | collective-permute-start | bytes 208904 | tf_op jit(solution)/shard_map/ppermute | solution.py:35
  42.2 6.7 %collective-permute-start.4 = (bf16[272,128]{0,1:T(8,128)(2,1)S(1)}, bf16[272,128]{0,1:T(8,128)(2,1)S(1)}, u32[]{:S(2)}, u32[]{:S(2)}) collective-permute-start(bf16[272,128]{0,1:T(8,128)(2,1)S(1)} %pad_maximum_fusion.2), channel_id=1, source_target_pairs={{0,80},{16,96},{32,112},{1,81},{17,97},{33,113},{2,82},{18,98},{34... | collective-permute-start | bytes 208904 | tf_op jit(solution)/shard_map/ppermute | solution.py:35
  42.9 6.0 %collective-permute-start.5 = (bf16[272,128]{0,1:T(8,128)(2,1)S(1)}, bf16[272,128]{0,1:T(8,128)(2,1)S(1)}, u32[]{:S(2)}, u32[]{:S(2)}) collective-permute-start(bf16[272,128]{0,1:T(8,128)(2,1)S(1)} %pad_maximum_fusion.2), channel_id=1, source_target_pairs={{0,96},{16,112},{1,97},{17,113},{2,98},{18,114},{3,99},{19,115},{4... | collective-permute-start | bytes 208904 | tf_op jit(solution)/shard_map/ppermute | solution.py:35
  44.4 4.9 %collective-permute-start.6 = (bf16[272,128]{0,1:T(8,128)(2,1)S(1)}, bf16[272,128]{0,1:T(8,128)(2,1)S(1)}, u32[]{:S(2)}, u32[]{:S(2)}) collective-permute-start(bf16[272,128]{0,1:T(8,128)(2,1)S(1)} %pad_maximum_fusion.2), channel_id=1, source_target_pairs={{0,112},{1,113},{2,114},{3,115},{4,116},{5,117},{6,118},{7,119},{8... | collective-permute-start | bytes 208904 | tf_op jit(solution)/shard_map/ppermute | solution.py:35
  52.0 3.9 %copy-start.14 = (s32[16,2]{0,1:T(2,128)S(1)}, s32[16,2]{0,1:T(2,128)}, u32[]{:S(2)}) copy-start(s32[16,2]{0,1:T(2,128)} %param.24) | copy-start | bytes 388
  52.0 45.1 %all-to-all-start = ((bf16[16,256,256]{2,1,0:T(8,128)(2,1)}), bf16[16,256,256]{2,1,0:T(8,128)(2,1)S(1)}, u32[]{:S(2)}, u32[]{:S(2)}) async-start(bf16[16,256,256]{2,1,0:T(8,128)(2,1)} %broadcast_in_dim.27), calls=%async_computation | async-start | bytes 4194304 | tf_op jit(solution)/shard_map/all_to_all | solution.py:39
  97.1 1.3 copy-start.2
  131.7 18.1 %collective-permute-start.7 = (bf16[48,6144]{1,0:T(8,128)(2,1)}, bf16[48,6144]{1,0:T(8,128)(2,1)S(1)}, u32[]{:S(2)}, u32[]{:S(2)}) collective-permute-start(bf16[48,6144]{1,0:T(8,128)(2,1)} %get-tuple-element.27.refs_0_), channel_id=1, source_target_pairs={{0,32},{16,48},{32,64},{48,80},{64,96},{80,112},{96,0},{112,16},{1... | collective-permute-start | bytes 1769480 | tf_op jit(solution)/shard_map/ppermute | solution.py:27
  139.1 12.7 %collective-permute-start.8 = (bf16[48,6144]{1,0:T(8,128)(2,1)}, bf16[48,6144]{1,0:T(8,128)(2,1)S(1)}, u32[]{:S(2)}, u32[]{:S(2)}) collective-permute-start(bf16[48,6144]{1,0:T(8,128)(2,1)} %get-tuple-element.27.refs_0_), channel_id=1, source_target_pairs={{0,96},{16,112},{32,0},{48,16},{64,32},{80,48},{96,64},{112,80},{1... | collective-permute-start | bytes 1769480 | tf_op jit(solution)/shard_map/ppermute | solution.py:27
  140.3 21.9 %collective-permute-start.10 = (bf16[48,6144]{1,0:T(8,128)(2,1)}, bf16[48,6144]{1,0:T(8,128)(2,1)S(1)}, u32[]{:S(2)}, u32[]{:S(2)}) collective-permute-start(bf16[48,6144]{1,0:T(8,128)(2,1)} %get-tuple-element.27.refs_0_), channel_id=1, source_target_pairs={{0,16},{16,0},{32,48},{48,32},{64,80},{80,64},{96,112},{112,96},{1... | collective-permute-start | bytes 1769480 | tf_op jit(solution)/shard_map/ppermute | solution.py:31
  146.9 16.5 %collective-permute-start.22 = (bf16[48,6144]{1,0:T(8,128)(2,1)}, bf16[48,6144]{1,0:T(8,128)(2,1)S(1)}, u32[]{:S(2)}, u32[]{:S(2)}) collective-permute-start(bf16[48,6144]{1,0:T(8,128)(2,1)} %get-tuple-element.36.refs_0_), channel_id=1, source_target_pairs={{0,96},{16,112},{32,0},{48,16},{64,32},{80,48},{96,64},{112,80},{1... | collective-permute-start | bytes 1769480 | tf_op jit(solution)/shard_map/ppermute | solution.py:27
  149.8 32.0 %copy-start.21 = (bf16[48,6144]{1,0:T(8,128)(2,1)}, bf16[48,6144]{1,0:T(8,128)(2,1)S(1)}, u32[]{:S(2)}) copy-start(bf16[48,6144]{1,0:T(8,128)(2,1)S(1)} %collective-permute-done.7.refs_1_) | copy-start | bytes 1769476
  149.8 15.7 %collective-permute-start.9 = (bf16[48,6144]{1,0:T(8,128)(2,1)S(1)}, bf16[48,6144]{1,0:T(8,128)(2,1)}, u32[]{:S(2)}, u32[]{:S(2)}) collective-permute-start(bf16[48,6144]{1,0:T(8,128)(2,1)S(1)} %collective-permute-done.7.refs_1_), channel_id=1, source_target_pairs={{0,32},{16,48},{32,64},{48,80},{64,96},{80,112},{96,0},{112,16},{1... | collective-permute-start | bytes 1769480 | tf_op jit(solution)/shard_map/ppermute | solution.py:27
  149.8 27.7 %collective-permute-start.21 = (bf16[48,6144]{1,0:T(8,128)(2,1)}, bf16[48,6144]{1,0:T(8,128)(2,1)S(1)}, u32[]{:S(2)}, u32[]{:S(2)}) collective-permute-start(bf16[48,6144]{1,0:T(8,128)(2,1)} %get-tuple-element.36.refs_0_), channel_id=1, source_target_pairs={{0,32},{16,48},{32,64},{48,80},{64,96},{80,112},{96,0},{112,16},{1... | collective-permute-start | bytes 1769480 | tf_op jit(solution)/shard_map/ppermute | solution.py:27
  151.8 30.1 %copy-start.22 = (bf16[48,6144]{1,0:T(8,128)(2,1)}, bf16[48,6144]{1,0:T(8,128)(2,1)S(1)}, u32[]{:S(2)}) copy-start(bf16[48,6144]{1,0:T(8,128)(2,1)S(1)} %collective-permute-done.8.refs_2_) | copy-start | bytes 1769476
  151.8 28.4 %collective-permute-start.11 = (bf16[48,6144]{1,0:T(8,128)(2,1)S(1)}, bf16[48,6144]{1,0:T(8,128)(2,1)}, u32[]{:S(2)}, u32[]{:S(2)}) collective-permute-start(bf16[48,6144]{1,0:T(8,128)(2,1)S(1)} %collective-permute-done.7.refs_1_), channel_id=1, source_target_pairs={{0,16},{16,0},{32,48},{48,32},{64,80},{80,64},{96,112},{112,96},{1... | collective-permute-start | bytes 1769480 | tf_op jit(solution)/shard_map/ppermute | solution.py:31
  162.2 19.7 %copy-start.23 = (bf16[48,6144]{1,0:T(8,128)(2,1)}, bf16[48,6144]{1,0:T(8,128)(2,1)S(1)}, u32[]{:S(2)}) copy-start(bf16[48,6144]{1,0:T(8,128)(2,1)S(1)} %collective-permute-done.10.refs_4_) | copy-start | bytes 1769476
  162.2 18.1 %collective-permute-start.12 = (bf16[48,6144]{1,0:T(8,128)(2,1)S(1)}, bf16[48,6144]{1,0:T(8,128)(2,1)}, u32[]{:S(2)}, u32[]{:S(2)}) collective-permute-start(bf16[48,6144]{1,0:T(8,128)(2,1)S(1)} %collective-permute-done.8.refs_2_), channel_id=1, source_target_pairs={{0,16},{16,0},{32,48},{48,32},{64,80},{80,64},{96,112},{112,96},{1... | collective-permute-start | bytes 1769480 | tf_op jit(solution)/shard_map/ppermute | solution.py:31
  163.3 39.4 %copy-start.18 = (bf16[48,6144]{1,0:T(8,128)(2,1)}, bf16[48,6144]{1,0:T(8,128)(2,1)S(1)}, u32[]{:S(2)}) copy-start(bf16[48,6144]{1,0:T(8,128)(2,1)S(1)} %collective-permute-done.22.refs_2_) | copy-start | bytes 1769476
  163.3 17.4 %collective-permute-start.23 = (bf16[48,6144]{1,0:T(8,128)(2,1)S(1)}, bf16[48,6144]{1,0:T(8,128)(2,1)}, u32[]{:S(2)}, u32[]{:S(2)}) collective-permute-start(bf16[48,6144]{1,0:T(8,128)(2,1)S(1)} %collective-permute-done.22.refs_2_), channel_id=1, source_target_pairs={{0,96},{16,112},{32,0},{48,16},{64,32},{80,48},{96,64},{112,80},{1... | collective-permute-start | bytes 1769480 | tf_op jit(solution)/shard_map/ppermute | solution.py:27
  165.5 16.3 %collective-permute-start.13 = (bf16[48,6144]{1,0:T(8,128)(2,1)}, bf16[48,6144]{1,0:T(8,128)(2,1)}, u32[]{:S(2)}, u32[]{:S(2)}) collective-permute-start(bf16[48,6144]{1,0:T(8,128)(2,1)} %collective-permute-done.9.refs_3_), channel_id=1, source_target_pairs={{0,16},{16,0},{32,48},{48,32},{64,80},{80,64},{96,112},{112,96},{1... | collective-permute-start | bytes 1769480 | tf_op jit(solution)/shard_map/ppermute | solution.py:31
  174.0 102.8 %all-to-all-start.2 = ((bf16[16,16,384]{2,1,0:T(8,128)(2,1)}), bf16[16,16,384]{2,1,0:T(8,128)(2,1)S(1)}, u32[]{:S(2)}, u32[]{:S(2)}) async-start(bf16[16,16,384]{2,1,0:T(8,128)(2,1)} %bitcast.22), calls=%async_computation.2 | async-start | bytes 393216 | tf_op jit(solution)/shard_map/all_to_all | solution.py:39
  177.5 25.2 %copy-start.19 = (bf16[48,6144]{1,0:T(8,128)(2,1)}, bf16[48,6144]{1,0:T(8,128)(2,1)S(1)}, u32[]{:S(2)}) copy-start(bf16[48,6144]{1,0:T(8,128)(2,1)S(1)} %collective-permute-done.21.refs_1_) | copy-start | bytes 1769476
  177.5 25.3 %collective-permute-start.24 = (bf16[48,6144]{1,0:T(8,128)(2,1)}, bf16[48,6144]{1,0:T(8,128)(2,1)S(1)}, u32[]{:S(2)}, u32[]{:S(2)}) collective-permute-start(bf16[48,6144]{1,0:T(8,128)(2,1)} %get-tuple-element.36.refs_0_), channel_id=1, source_target_pairs={{0,16},{16,0},{32,48},{48,32},{64,80},{80,64},{96,112},{112,96},{1... | collective-permute-start | bytes 1769480 | tf_op jit(solution)/shard_map/ppermute | solution.py:31
  180.2 23.3 %collective-permute-start.26 = (bf16[48,6144]{1,0:T(8,128)(2,1)S(1)}, bf16[48,6144]{1,0:T(8,128)(2,1)S(1)}, u32[]{:S(2)}, u32[]{:S(2)}) collective-permute-start(bf16[48,6144]{1,0:T(8,128)(2,1)S(1)} %collective-permute-done.22.refs_2_), channel_id=1, source_target_pairs={{0,16},{16,0},{32,48},{48,32},{64,80},{80,64},{96,112},{112,96},{1... | collective-permute-start | bytes 1769480 | tf_op jit(solution)/shard_map/ppermute | solution.py:31
  180.3 23.1 %collective-permute-start.25 = (bf16[48,6144]{1,0:T(8,128)(2,1)S(1)}, bf16[48,6144]{1,0:T(8,128)(2,1)S(1)}, u32[]{:S(2)}, u32[]{:S(2)}) collective-permute-start(bf16[48,6144]{1,0:T(8,128)(2,1)S(1)} %collective-permute-done.21.refs_1_), channel_id=1, source_target_pairs={{0,16},{16,0},{32,48},{48,32},{64,80},{80,64},{96,112},{112,96},{1... | collective-permute-start | bytes 1769480 | tf_op jit(solution)/shard_map/ppermute | solution.py:31
  180.7 23.2 %collective-permute-start.27 = (bf16[48,6144]{1,0:T(8,128)(2,1)}, bf16[48,6144]{1,0:T(8,128)(2,1)S(1)}, u32[]{:S(2)}, u32[]{:S(2)}) collective-permute-start(bf16[48,6144]{1,0:T(8,128)(2,1)} %collective-permute-done.23.refs_3_), channel_id=1, source_target_pairs={{0,16},{16,0},{32,48},{48,32},{64,80},{80,64},{96,112},{112,96},{1... | collective-permute-start | bytes 1769480 | tf_op jit(solution)/shard_map/ppermute | solution.py:31
  202.8 23.7 %collective-permute-start.16 = (bf16[48,6144]{1,0:T(8,128)(2,1)}, bf16[48,6144]{1,0:T(8,128)(2,1)S(1)}, u32[]{:S(2)}, u32[]{:S(2)}) collective-permute-start(bf16[48,6144]{1,0:T(8,128)(2,1)} %get-tuple-element.33), channel_id=1, source_target_pairs={{0,16},{16,0},{32,48},{48,32},{64,80},{80,64},{96,112},{112,96},{1... | collective-permute-start | bytes 1769480 | tf_op jit(solution)/shard_map/ppermute | solution.py:31
  202.9 27.9 %collective-permute-start.15 = (bf16[48,6144]{1,0:T(8,128)(2,1)}, bf16[48,6144]{1,0:T(8,128)(2,1)S(1)}, u32[]{:S(2)}, u32[]{:S(2)}) collective-permute-start(bf16[48,6144]{1,0:T(8,128)(2,1)} %get-tuple-element.31), channel_id=1, source_target_pairs={{0,16},{16,0},{32,48},{48,32},{64,80},{80,64},{96,112},{112,96},{1... | collective-permute-start | bytes 1769480 | tf_op jit(solution)/shard_map/ppermute | solution.py:31
  203.4 23.5 %collective-permute-start.19 = (bf16[48,6144]{1,0:T(8,128)(2,1)}, bf16[48,6144]{1,0:T(8,128)(2,1)S(1)}, u32[]{:S(2)}, u32[]{:S(2)}) collective-permute-start(bf16[48,6144]{1,0:T(8,128)(2,1)} %get-tuple-element.35), channel_id=1, source_target_pairs={{0,16},{16,0},{32,48},{48,32},{64,80},{80,64},{96,112},{112,96},{1... | collective-permute-start | bytes 1769480 | tf_op jit(solution)/shard_map/ppermute | solution.py:31
  203.5 23.2 %copy-start.4 = (bf16[48,6144]{1,0:T(8,128)(2,1)S(1)}, bf16[48,6144]{1,0:T(8,128)(2,1)}, u32[]{:S(2)}) copy-start(bf16[48,6144]{1,0:T(8,128)(2,1)} %get-tuple-element.32) | copy-start | bytes 1769476
  203.5 57.0 %collective-permute-start.14 = (bf16[48,6144]{1,0:T(8,128)(2,1)}, bf16[48,6144]{1,0:T(8,128)(2,1)S(1)}, u32[]{:S(2)}, u32[]{:S(2)}) collective-permute-start(bf16[48,6144]{1,0:T(8,128)(2,1)} %get-tuple-element.29), channel_id=1, source_target_pairs={{0,16},{16,0},{32,48},{48,32},{64,80},{80,64},{96,112},{112,96},{1... | collective-permute-start | bytes 1769480 | tf_op jit(solution)/shard_map/ppermute | solution.py:31
  226.1 1.1 copy-start.25
  226.1 1.4 copy-start.3
  226.1 2.3 collective-permute-start.29
  226.5 2.7 collective-permute-start.32
  226.8 1.6 copy-start.20
  226.8 1.9 copy-start.6
  227.1 20.3 %collective-permute-start.31 = (bf16[48,6144]{1,0:T(8,128)(2,1)S(1)}, bf16[48,6144]{1,0:T(8,128)(2,1)S(1)}, u32[]{:S(2)}, u32[]{:S(2)}) collective-permute-start(bf16[48,6144]{1,0:T(8,128)(2,1)S(1)} %copy-done.25), channel_id=1, source_target_pairs={{0,16},{16,0},{32,48},{48,32},{64,80},{80,64},{96,112},{112,96},{1... | collective-permute-start | bytes 1769480 | tf_op jit(solution)/shard_map/ppermute | solution.py:31
  227.6 3.1 copy-start.5
  228.4 45.9 %collective-permute-start.28 = (bf16[48,6144]{1,0:T(8,128)(2,1)S(1)}, bf16[48,6144]{1,0:T(8,128)(2,1)S(1)}, u32[]{:S(2)}, u32[]{:S(2)}) collective-permute-start(bf16[48,6144]{1,0:T(8,128)(2,1)S(1)} %copy-done.20), channel_id=1, source_target_pairs={{0,16},{16,0},{32,48},{48,32},{64,80},{80,64},{96,112},{112,96},{1... | collective-permute-start | bytes 1769480 | tf_op jit(solution)/shard_map/ppermute | solution.py:31
  228.9 18.4 %copy-start.9 = (bf16[48,6144]{1,0:T(8,128)(2,1)S(1)}, bf16[48,6144]{1,0:T(8,128)(2,1)}, u32[]{:S(2)}) copy-start(bf16[48,6144]{1,0:T(8,128)(2,1)} %get-tuple-element.30) | copy-start | bytes 1769476
  229.2 15.7 %collective-permute-start.17 = (bf16[48,6144]{1,0:T(8,128)(2,1)S(1)}, bf16[48,6144]{1,0:T(8,128)(2,1)S(1)}, u32[]{:S(2)}, u32[]{:S(2)}) collective-permute-start(bf16[48,6144]{1,0:T(8,128)(2,1)S(1)} %add_convert_fusion.7), channel_id=1, source_target_pairs={{0,32},{16,48},{32,64},{48,80},{64,96},{80,112},{96,0},{112,16},{1... | collective-permute-start | bytes 1769480 | tf_op jit(solution)/shard_map/ppermute | solution.py:27
  230.8 30.5 %collective-permute-start.20 = (bf16[48,6144]{1,0:T(8,128)(2,1)S(1)}, bf16[48,6144]{1,0:T(8,128)(2,1)S(1)}, u32[]{:S(2)}, u32[]{:S(2)}) collective-permute-start(bf16[48,6144]{1,0:T(8,128)(2,1)S(1)} %add_convert_fusion.5), channel_id=1, source_target_pairs={{0,96},{16,112},{32,0},{48,16},{64,32},{80,48},{96,64},{112,80},{1... | collective-permute-start | bytes 1769480 | tf_op jit(solution)/shard_map/ppermute | solution.py:27
  244.9 14.1 %collective-permute-start.33 = (bf16[48,6144]{1,0:T(8,128)(2,1)S(1)}, bf16[48,6144]{1,0:T(8,128)(2,1)S(1)}, u32[]{:S(2)}, u32[]{:S(2)}) collective-permute-start(bf16[48,6144]{1,0:T(8,128)(2,1)S(1)} %add_convert_fusion.2), channel_id=1, source_target_pairs={{0,96},{16,112},{32,0},{48,16},{64,32},{80,48},{96,64},{112,80},{1... | collective-permute-start | bytes 1769480 | tf_op jit(solution)/shard_map/ppermute | solution.py:27
  247.2 13.0 %copy-start.10 = (bf16[48,6144]{1,0:T(8,128)(2,1)S(1)}, bf16[48,6144]{1,0:T(8,128)(2,1)}, u32[]{:S(2)}) copy-start(bf16[48,6144]{1,0:T(8,128)(2,1)} %get-tuple-element.41) | copy-start | bytes 1769476
  247.5 26.8 %collective-permute-start.30 = (bf16[48,6144]{1,0:T(8,128)(2,1)S(1)}, bf16[48,6144]{1,0:T(8,128)(2,1)S(1)}, u32[]{:S(2)}, u32[]{:S(2)}) collective-permute-start(bf16[48,6144]{1,0:T(8,128)(2,1)S(1)} %add_convert_fusion.3), channel_id=1, source_target_pairs={{0,32},{16,48},{32,64},{48,80},{64,96},{80,112},{96,0},{112,16},{1... | collective-permute-start | bytes 1769480 | tf_op jit(solution)/shard_map/ppermute | solution.py:27
  259.0 15.0 %collective-permute-start.18 = (bf16[48,6144]{1,0:T(8,128)(2,1)S(1)}, bf16[48,6144]{1,0:T(8,128)(2,1)S(1)}, u32[]{:S(2)}, u32[]{:S(2)}) collective-permute-start(bf16[48,6144]{1,0:T(8,128)(2,1)S(1)} %add_convert_fusion.6), channel_id=1, source_target_pairs={{0,32},{16,48},{32,64},{48,80},{64,96},{80,112},{96,0},{112,16},{1... | collective-permute-start | bytes 1769480 | tf_op jit(solution)/shard_map/ppermute | solution.py:27
  260.2 13.7 %copy-start.7 = (bf16[48,6144]{1,0:T(8,128)(2,1)S(1)}, bf16[48,6144]{1,0:T(8,128)(2,1)}, u32[]{:S(2)}) copy-start(bf16[48,6144]{1,0:T(8,128)(2,1)} %get-tuple-element.28) | copy-start | bytes 1769476
  260.5 13.8 %collective-permute-start.34 = (bf16[48,6144]{1,0:T(8,128)(2,1)S(1)}, bf16[48,6144]{1,0:T(8,128)(2,1)S(1)}, u32[]{:S(2)}, u32[]{:S(2)}) collective-permute-start(bf16[48,6144]{1,0:T(8,128)(2,1)S(1)} %add_convert_fusion.1), channel_id=1, source_target_pairs={{0,96},{16,112},{32,0},{48,16},{64,32},{80,48},{96,64},{112,80},{1... | collective-permute-start | bytes 1769480 | tf_op jit(solution)/shard_map/ppermute | solution.py:27
  274.0 1.1 copy-start.8
  276.8 4.5 %copy-start.17 = (s32[16,2]{0,1:T(2,128)S(1)}, s32[16,2]{0,1:T(2,128)}, u32[]{:S(2)}) copy-start(s32[16,2]{0,1:T(2,128)} %param.25) | copy-start | bytes 388
  276.8 24.7 %all-to-all-start.4 = ((bf16[16,6,6144]{2,1,0:T(8,128)(2,1)}), bf16[16,6,6144]{2,1,0:T(8,128)(2,1)S(1)}, u32[]{:S(2)}, u32[]{:S(2)}) async-start(bf16[16,6,6144]{2,1,0:T(8,128)(2,1)} %reshape.521), calls=%async_computation.4 | async-start | bytes 3145728 | tf_op jit(solution)/shard_map/all_to_all | solution.py:39
  303.1 5.4 %copy-start.1 = (bf16[256,6144]{1,0:T(8,128)(2,1)S(1)}, bf16[256,6144]{1,0:T(8,128)(2,1)}, u32[]{:S(2)}) copy-start(bf16[256,6144]{1,0:T(8,128)(2,1)} %param.18) | copy-start | bytes 9437188
  (5 other events, 4.3 us)
Sparse Core Ops, SparseCore 0:
  30.4 31.4 all-gather.3
